TPU v7x, 32 devices: a whole 2x2x4 slice. The times are simulated.
32 devices in a mesh: row: 4 (over z), col: 8 (over y, x, core).
Axes of the slice: x: 2, y: 2, z: 4, core: 2. Of those that a mesh axis runs over, the one named last changes fastest.
Arguments:
- primal: float32 [8, 32768], P(None, ('col', 'row')), may hold values from 0 to 0.5
- dual: float32 [8, 32768], P(None, ('row', 'col')), may hold values from 0 to 1
- cost: float32 [8, 32768], P(None, ('col', 'row')), may hold values from -6 to 6
- upper: float32 [32768], P(('col', 'row')), may hold values from 0.25 to 1.5
- rhs: float32 [32768], P(('row', 'col')), may hold values from -6 to 6
- row_kind: int32 [32768], P(('row', 'col')), may hold values 0 or 1
- tiles: bfloat16 [1536, 128, 128], P(('row', 'col')), may hold values from -0.25 to 0.25
- tile_rows: int32 [1536], P(('row', 'col')), may hold values from 0 to 63, as said below
- tile_cols: int32 [1536], P(('row', 'col')), may hold values from 0 to 31
- tile_count: int32 [32], P(('row', 'col')), may hold values from 1 to 48, as said below
Outputs:
- primal_out: float32 [8, 32768], P(None, ('col', 'row'))
- dual_out: float32 [8, 32768], P(None, ('row', 'col'))
Inputs may be any that keep to these rules, and one draw needn't show every extreme that they name: Within one device's slots the pairs (tile_rows, tile_cols) are all different. `tile_count`: some device has all 48 slots live in every draw; which one varies.
All inputs are finite; a program needn't handle non-finite values. No bound on the sum of `row_kind` on one device may be relied on, other than what follows from the above.
Results may differ from a plain program's by a relative error of at most 0.0012.
Values may be sent and summed in bfloat16 or wider, within the bound.
A program may use at most 64 MiB of HBM per device.

v0:
```python
import jax
import jax.numpy as jnp
from jax import lax
from jax.sharding import PartitionSpec as P

ITERS = 2


PRIMAL_STEP = 0.4
DUAL_STEP = 0.4


def tile_forward(source, tiles, tile_rows, tile_cols, live, row_tiles):
    width = source.shape[0]
    col_tiles = source.shape[1] // 128
    pieces = source.reshape(width, col_tiles, 128)[:, tile_cols]
    contrib = jnp.einsum("rtk,tjk->rtj", pieces, tiles, preferred_element_type=jnp.float32)
    onehot = (
        (tile_rows[:, None] == jnp.arange(row_tiles, dtype=jnp.int32)[None, :]) & live[:, None]
    ).astype(jnp.float32)
    return jnp.einsum("rtj,ts->rsj", contrib, onehot, precision=lax.Precision.HIGHEST).reshape(
        width, row_tiles * 128
    )


def tile_adjoint(source, tiles, tile_rows, tile_cols, live, col_tiles):
    width = source.shape[0]
    row_tiles = source.shape[1] // 128
    pieces = source.reshape(width, row_tiles, 128)[:, tile_rows]
    contrib = jnp.einsum("rtj,tjk->rtk", pieces, tiles, preferred_element_type=jnp.float32)
    onehot = (
        (tile_cols[:, None] == jnp.arange(col_tiles, dtype=jnp.int32)[None, :]) & live[:, None]
    ).astype(jnp.float32)
    return jnp.einsum("rtk,ts->rsk", contrib, onehot, precision=lax.Precision.HIGHEST).reshape(
        width, col_tiles * 128
    )


def body(primal, dual, cost, upper, rhs, row_kind, tiles, tile_rows, tile_cols, tile_count):
    row_devices = lax.axis_size("row")
    col_devices = lax.axis_size("col")
    primal_width = primal.shape[1]
    dual_width = dual.shape[1]
    col_tiles = primal_width * row_devices // 128
    row_tiles = dual_width * col_devices // 128
    live = jnp.arange(tiles.shape[0], dtype=jnp.int32) < tile_count[0]
    kind_float = row_kind.astype(jnp.float32)
    state_x, cost_here, upper_here = (primal, cost, upper)
    state_y, rhs_here, kind_here = (dual, rhs, kind_float)
    for step in range(ITERS):
        dual_low = state_y.astype(jnp.bfloat16)
        dual_rows = lax.all_gather(dual_low, "col", axis=1, tiled=True)
        partial_grad = tile_adjoint(dual_rows, tiles, tile_rows, tile_cols, live, col_tiles)
        grad_part = lax.psum_scatter(partial_grad, "row", scatter_dimension=1, tiled=True)
        x_new = jnp.clip(state_x - PRIMAL_STEP * (cost_here - grad_part), 0.0, upper_here[None, :])
        xbar = (2.0 * x_new - state_x).astype(jnp.bfloat16)
        xbar_block = lax.all_gather(xbar, "row", axis=1, tiled=True)
        partial_image = tile_forward(xbar_block, tiles, tile_rows, tile_cols, live, row_tiles)
        image = lax.psum_scatter(partial_image, "col", scatter_dimension=1, tiled=True)
        y_new = state_y + DUAL_STEP * (rhs_here[None, :] - image)
        y_new = jnp.where(kind_here[None, :] > 0.5, jnp.maximum(y_new, 0.0), y_new)
        state_x = x_new
        state_y = y_new
    return (state_x, state_y)


def solution(mesh):
    in_specs = (
        P(None, ("col", "row")),
        P(None, ("row", "col")),
        P(None, ("col", "row")),
        P(("col", "row")),
        P(("row", "col")),
        P(("row", "col")),
        P(("row", "col"), None, None),
        P(("row", "col")),
        P(("row", "col")),
        P(("row", "col")),
    )
    out_specs = (P(None, ("col", "row")), P(None, ("row", "col")))
    return jax.shard_map(body, mesh=mesh, in_specs=in_specs, out_specs=out_specs, check_vma=False)
```

profile of v0, /device:TPU:0, one launch (start us, length us, event | category | flops | bytes accessed | tf_op | source)
XLA Modules:
  0.0 179.2 jit_solution(10547060907542990384)
XLA Ops:
  7.2 0.0 copy-start
  7.2 0.0 copy-start.8
  7.2 0.0 copy-start.5
  7.2 0.0 copy-start.2
  7.2 0.0 copy-start.4
  7.2 0.0 reduce-scatter.5.cloned.1.call-start
  8.0 0.7 compare_select_fusion.1
  8.7 0.8 convert_element_type.19
  9.5 10.7 %all_gather.12 = bf16[8,8192]{1,0:T(8,128)(2,1)S(1)} all-gather(bf16[8,1024]{1,0:T(8,128)(2,1)S(1)} %convert_element_type.19), channel_id=1, replica_groups=mesh['row'=4,'col'=8] {'col'}, dimensions={1}, use_global_device_ids=true | all-gather | bytes 147456 | tf_op jit(solution)/shard_map/all_gather | solution.py:52
  20.1 0.6 gather_fusion
  20.7 0.0 copy-done
  20.7 0.5 fusion.14
  21.3 0.0 copy-done.8
  21.3 0.0 copy-start.9
  21.3 0.2 convolution_bitcast_fusion.3
  21.5 0.7 copy.43
  22.2 0.0 reduce-scatter.5.cloned.1.call-update
  22.2 0.0 reduce-scatter.7.cloned.1.call-start
  22.3 19.6 %reduce-scatter.5.cloned.1.call-done = f32[8,1024]{1,0:T(8,128)} async-done(((f32[8,4096]{1,0:T(8,128)}), f32[8,1024]{1,0:T(8,128)}) %reduce-scatter.5.cloned.1.call-update) | async-done | bytes 32784 | tf_op jit(solution)/shard_map/reduce_scatter | solution.py:54
  41.9 0.0 copy-done.5
  41.9 0.0 copy-done.2
  41.9 0.0 copy-done.4
  41.9 0.8 subtract_convert_fusion.1
  42.7 13.1 %all_gather.13 = bf16[8,4096]{1,0:T(8,128)(2,1)S(1)} all-gather(bf16[8,1024]{1,0:T(8,128)(2,1)S(1)} %get-tuple-element.4), channel_id=1, replica_groups=mesh['row'=4,'col'=8] {'row'}, dimensions={1}, use_global_device_ids=true | all-gather | bytes 81920 | tf_op jit(solution)/shard_map/all_gather | solution.py:57
  55.8 0.6 gather_fusion.1
  56.4 0.0 copy-start.7
  56.4 0.0 copy-start.1
  56.4 0.0 copy-start.6
  56.5 0.9 fusion.12
  57.4 0.0 copy-done.9
  57.4 0.4 convolution_bitcast_fusion.1
  57.8 0.9 copy.41
  58.6 0.0 reduce-scatter.7.cloned.1.call-update
  58.7 0.0 reduce-scatter.9.cloned.1.call-start
  58.7 0.0 copy-done.7
  58.7 31.9 %reduce-scatter.7.cloned.1.call-done = f32[8,1024]{1,0:T(8,128)} async-done(((f32[8,8192]{1,0:T(8,128)}), f32[8,1024]{1,0:T(8,128)}) %reduce-scatter.7.cloned.1.call-update) | async-done | bytes 32784 | tf_op jit(solution)/shard_map/reduce_scatter | solution.py:59
  90.6 0.0 copy-done.1
  90.6 0.0 copy-done.6
  90.6 0.8 fusion.32
  91.4 9.2 %all_gather.14 = bf16[8,8192]{1,0:T(8,128)(2,1)S(1)} all-gather(bf16[8,1024]{1,0:T(8,128)(2,1)S(1)} %fusion.32), channel_id=1, replica_groups=mesh['row'=4,'col'=8] {'col'}, dimensions={1}, use_global_device_ids=true | all-gather | bytes 147456 | tf_op jit(solution)/shard_map/all_gather | solution.py:52
  100.5 0.6 gather_fusion.2
  101.2 0.5 fusion.10
  101.7 0.2 convolution_bitcast_fusion.2
  101.9 0.7 copy.42
  102.6 0.0 reduce-scatter.9.cloned.1.call-update
  102.7 0.0 reduce-scatter.11.cloned.1.call-start
  102.7 19.3 %reduce-scatter.9.cloned.1.call-done = f32[8,1024]{1,0:T(8,128)} async-done(((f32[8,4096]{1,0:T(8,128)}), f32[8,1024]{1,0:T(8,128)}) %reduce-scatter.9.cloned.1.call-update) | async-done | bytes 32784 | tf_op jit(solution)/shard_map/reduce_scatter | solution.py:54
  122.0 1.4 subtract_convert_fusion
  123.4 13.1 %all_gather.15 = bf16[8,4096]{1,0:T(8,128)(2,1)S(1)} all-gather(bf16[8,1024]{1,0:T(8,128)(2,1)S(1)} %get-tuple-element.2), channel_id=1, replica_groups=mesh['row'=4,'col'=8] {'row'}, dimensions={1}, use_global_device_ids=true | all-gather | bytes 81920 | tf_op jit(solution)/shard_map/all_gather | solution.py:57
  136.5 0.6 gather_fusion.3
  137.1 0.0 copy-start.3
  137.1 0.9 fusion.8
  138.0 0.4 convolution_bitcast_fusion
  138.4 0.9 copy.40
  139.3 0.0 reduce-scatter.11.cloned.1.call-update
  139.3 31.9 %reduce-scatter.11.cloned.1.call-done = f32[8,1024]{1,0:T(8,128)} async-done(((f32[8,8192]{1,0:T(8,128)}), f32[8,1024]{1,0:T(8,128)}) %reduce-scatter.11.cloned.1.call-update) | async-done | bytes 32784 | tf_op jit(solution)/shard_map/reduce_scatter | solution.py:59
  171.2 0.0 copy-done.3
  171.2 1.4 maximum_select_fusion
  (5 shorter events, 0.0 us)
Async XLA Ops:
  7.2 13.6 %copy-start = (bf16[48,128,128]{2,1,0:T(8,128)(2,1)S(1)}, bf16[48,128,128]{2,1,0:T(8,128)(2,1)}, u32[]{:S(2)}) copy-start(bf16[48,128,128]{2,1,0:T(8,128)(2,1)} %param.16) | copy-start | bytes 4718596
  7.2 14.1 %copy-start.8 = (s32[48]{0:T(128)S(1)}, s32[48]{0:T(128)}, u32[]{:S(2)}) copy-start(s32[48]{0:T(128)} %param.18) | copy-start | bytes 580
  7.2 34.7 %copy-start.5 = (f32[1024]{0:T(1024)S(1)}, f32[1024]{0:T(1024)}, u32[]{:S(2)}) copy-start(f32[1024]{0:T(1024)} %param.13) | copy-start | bytes 12292
  7.2 34.7 %copy-start.2 = (f32[8,1024]{1,0:T(8,128)S(1)}, f32[8,1024]{1,0:T(8,128)}, u32[]{:S(2)}) copy-start(f32[8,1024]{1,0:T(8,128)} %param.12) | copy-start | bytes 98308
  7.2 34.7 %copy-start.4 = (f32[8,1024]{1,0:T(8,128)S(1)}, f32[8,1024]{1,0:T(8,128)}, u32[]{:S(2)}) copy-start(f32[8,1024]{1,0:T(8,128)} %param.10) | copy-start | bytes 98308
  7.2 34.7 %reduce-scatter.5.cloned.1.call-start = ((), (), s32[]{:S(2)}) async-start(), calls=%async_computation.4 | async-start | bytes 163840 | tf_op jit(solution)/shard_map/reduce_scatter | solution.py:54
  21.3 36.1 %copy-start.9 = (s32[48]{0:T(128)S(1)}, s32[48]{0:T(128)}, u32[]{:S(2)}) copy-start(s32[48]{0:T(128)} %param.17) | copy-start | bytes 580
  22.2 68.3 %reduce-scatter.7.cloned.1.call-start = ((), (), s32[]{:S(2)}) async-start(), calls=%async_computation.5 | async-start | bytes 294912 | tf_op jit(solution)/shard_map/reduce_scatter | solution.py:59
  56.4 2.3 %copy-start.7 = (s32[1024]{0:T(1024)S(1)}, s32[1024]{0:T(1024)}, u32[]{:S(2)}) copy-start(s32[1024]{0:T(1024)} %param.15) | copy-start | bytes 12292
  56.4 34.2 %copy-start.1 = (f32[8,1024]{1,0:T(8,128)S(1)}, f32[8,1024]{1,0:T(8,128)}, u32[]{:S(2)}) copy-start(f32[8,1024]{1,0:T(8,128)} %param.11) | copy-start | bytes 98308
  56.4 34.1 %copy-start.6 = (f32[1024]{0:T(1024)S(1)}, f32[1024]{0:T(1024)}, u32[]{:S(2)}) copy-start(f32[1024]{0:T(1024)} %param.14) | copy-start | bytes 12292
  58.7 63.3 %reduce-scatter.9.cloned.1.call-start = ((), (), s32[]{:S(2)}) async-start(), calls=%async_computation.6 | async-start | bytes 163840 | tf_op jit(solution)/shard_map/reduce_scatter | solution.py:54
  102.7 68.6 %reduce-scatter.11.cloned.1.call-start = ((), (), s32[]{:S(2)}) async-start(), calls=%async_computation.7 | async-start | bytes 294912 | tf_op jit(solution)/shard_map/reduce_scatter | solution.py:59
  137.1 34.1 %copy-start.3 = (f32[8,1024]{1,0:T(8,128)S(1)}, f32[8,1024]{1,0:T(8,128)}, u32[]{:S(2)}) copy-start(f32[8,1024]{1,0:T(8,128)} %reduce-scatter.7.cloned.1.call-done) | copy-start | bytes 98308
Sparse Core Ops, SparseCore 0:
  22.4 19.4 reduce-scatter.4
  58.8 31.7 reduce-scatter.6
  102.8 19.1 reduce-scatter.8
  139.4 31.7 reduce-scatter.10
where the time goes:
time: 180 us; the launch traced here: 179 us
  waiting for transfers between devices  103 us (57%)
  blocking collectives  46.1 us (26%)
  between operations  14.7 us (8%)
  other arithmetic  5.77 us (3%)
  local copies, waits for them, and re-layouts  5.67 us (3%)
  matrix products  4.09 us (2%)
    reduce_scatter x2, waiting for transfers between devices, body(): lax.psum_scatter(partial_image, 'col', scatter_dimension=1, tiled=True)  63.8 us
    reduce_scatter x2, waiting for transfers between devices, body(): lax.psum_scatter(partial_grad, 'row', scatter_dimension=1, tiled=True)  38.9 us
    all_gather x2, blocking collectives, body(): xbar_block = lax.all_gather(xbar, 'row', axis=1, tiled=True)  26.2 us
    all_gather x2, blocking collectives, body(): dual_rows = lax.all_gather(dual_low, 'col', axis=1, tiled=True)  19.8 us
  transfers between devices with their start and end apart: 4, of which 4 were waited for; matrix products, arithmetic and copies ran while one was open for 0% of the time, Pallas kernels for 0%

commit v1 on v0

v1 whole, which is shorter than its diff:
```python
import functools

import jax
import jax.numpy as jnp
from jax import lax
from jax.experimental import pallas as pl
from jax.experimental.pallas import tpu as pltpu
from jax.sharding import PartitionSpec as P

ITERS = 2
PRIMAL_STEP = 0.4
DUAL_STEP = 0.4
BF16 = jnp.bfloat16
F32 = jnp.float32


def kernel(
    n_row, n_col,
    primal_h, dual_h, cost_h, upper_h, rhs_h, kind_h, tiles_h, rows_h, cols_h, count_s, rows_s, cols_s,
    out_x_h, out_y_h,
    x_v, y_v, cost_v, upper_v, rhs_v, kind_v, tiles_v, rows_v, cols_v,
    spread_g, spread_h, contrib,
    y_send, y_recv, y_full, x_send, x_recv, x_full,
    g_send, g_recv, h_send, h_recv,
    in_sem, out_sem, ys_sem, yr_sem, gs_sem, gr_sem, xs_sem, xr_sem, hs_sem, hr_sem,
):
    me_i = lax.axis_index("row")
    me_j = lax.axis_index("col")
    slots = tiles_v.shape[0]
    x_tiles = x_v.shape[1] // 128
    y_tiles = y_v.shape[1] // 128
    x_rows, y_rows = x_tiles * 8, y_tiles * 8

    barrier = pltpu.get_barrier_semaphore()
    for d in range(1, n_col):
        pl.semaphore_signal(barrier, inc=1, device_id={"col": lax.rem(me_j + d, n_col)}, device_id_type=pl.DeviceIdType.MESH)
    for d in range(1, n_row):
        pl.semaphore_signal(barrier, inc=1, device_id={"row": lax.rem(me_i + d, n_row)}, device_id_type=pl.DeviceIdType.MESH)

    loads = [
        pltpu.make_async_copy(src, dst, in_sem.at[k])
        for k, (src, dst) in enumerate((
            (dual_h, y_v), (cols_h, cols_v), (rows_h, rows_v), (tiles_h, tiles_v), (primal_h, x_v),
            (cost_h, cost_v), (upper_h, upper_v), (rhs_h, rhs_v), (kind_h, kind_v),
        ))
    ]
    for load in loads:
        load.start()
    load_dual, load_cols, load_rows, load_tiles = loads[:4]
    load_rest = loads[4:]

    sends = []

    def push(src, dst, send_sem, recv_sem, device):
        copy = pltpu.make_async_remote_copy(
            src_ref=src, dst_ref=dst, send_sem=send_sem, recv_sem=recv_sem,
            device_id=device, device_id_type=pl.DeviceIdType.MESH,
        )
        copy.start()
        sends.append(copy)

    def gather_start(it, value, tiles, send, recv, full, me, n, axis, s_sem, r_sem):
        rows = tiles * 8
        for t in range(0, tiles, 2):
            pair = jnp.concatenate([value(t), value(t + 1)], axis=0).astype(BF16)
            send[it, t * 8:(t + 2) * 8, :] = pair
            wide = pair.astype(F32)
            full[it, me * tiles + t] = wide[:8]
            full[it, me * tiles + t + 1] = wide[8:]
        for d in range(1, n):
            push(
                send.at[it], recv.at[it, pl.ds(pl.multiple_of(me * rows, 16), rows), :],
                s_sem.at[it, d - 1], r_sem.at[it, d - 1], {axis: lax.rem(me + d, n)},
            )

    def gather_wait(it, tiles, send, recv, full, me, n, axis, s_sem, r_sem):
        rows = tiles * 8
        for d in range(1, n):
            src = lax.rem(me + n - d, n)
            place = recv.at[it, pl.ds(pl.multiple_of(src * rows, 16), rows), :]
            pltpu.make_async_remote_copy(
                src_ref=send.at[it], dst_ref=place, send_sem=s_sem.at[it, d - 1], recv_sem=r_sem.at[it, d - 1],
                device_id={axis: src}, device_id_type=pl.DeviceIdType.MESH,
            ).wait_recv()
            full[it, pl.ds(src * tiles, tiles)] = place[...].astype(F32).reshape(tiles, 8, 128)

    def products(it, full, index, contract):
        for s in range(0, slots, 2):
            parts = []
            for k in (s, s + 1):
                piece = full[it, index[k]].astype(BF16)
                parts.append(lax.dot_general(
                    piece, tiles_v[k], (((1,), (contract,)), ((), ())), preferred_element_type=F32,
                ))
            both = jnp.concatenate(parts, axis=0)
            high = both.astype(BF16)
            contrib[s * 8:(s + 2) * 8, :128] = high
            contrib[s * 8:(s + 2) * 8, 128:] = (both - high.astype(F32)).astype(BF16)

    def spread(matrix, block, rows):
        part = matrix[pl.ds(pl.multiple_of(block * rows, 16), rows), :]
        total = jnp.dot(part, contrib[...], preferred_element_type=F32)
        return total[:, :128] + total[:, 128:]

    def scatter_sum(it, matrix, rows, send, recv, me, n, axis, s_sem, r_sem):
        for d in range(1, n):
            target = lax.rem(me + d, n)
            send[it, d - 1] = spread(matrix, target, rows)
            push(send.at[it, d - 1], recv.at[it, d - 1], s_sem.at[it, d - 1], r_sem.at[it, d - 1], {axis: target})
        total = spread(matrix, me, rows)
        for d in range(1, n):
            pltpu.make_async_remote_copy(
                src_ref=send.at[it, d - 1], dst_ref=recv.at[it, d - 1], send_sem=s_sem.at[it, d - 1],
                recv_sem=r_sem.at[it, d - 1], device_id={axis: lax.rem(me + d, n)},
                device_id_type=pl.DeviceIdType.MESH,
            ).wait_recv()
            total = total + recv[it, d - 1]
        return total

    lanes = slots * 8

    def build(index_v, matrix):
        slot = lax.broadcasted_iota(jnp.int32, (8, slots), 1)
        place = jnp.where(slot < count_s[0], jnp.broadcast_to(index_v[...], (8, slots)), -1)
        lane = lax.broadcasted_iota(jnp.int32, (slots, lanes), 1)
        wider = (lane // 8 == lax.broadcasted_iota(jnp.int32, (slots, lanes), 0)).astype(F32).astype(BF16)
        place = jnp.dot(place.astype(F32).astype(BF16), wider, preferred_element_type=F32)
        own = lax.broadcasted_iota(jnp.int32, (8, lanes), 1) % 8 == lax.broadcasted_iota(jnp.int32, (8, lanes), 0)
        place = jnp.where(own, place, -1.0).astype(jnp.int32)
        two = jnp.concatenate([place, place - 1], axis=0)

        def step(c, carry):
            matrix[pl.ds(pl.multiple_of(c * 16, 16), 16), :] = jnp.where(two == 2 * c, 1.0, 0.0).astype(BF16)
            return carry

        lax.fori_loop(0, matrix.shape[0] // 16, step, 0)

    load_dual.wait()
    pl.semaphore_wait(barrier, n_row + n_col - 2)
    for it in range(ITERS):
        last = it == ITERS - 1
        y_args = (y_tiles, y_send, y_recv, y_full, me_j, n_col, "col", ys_sem, yr_sem)
        gather_start(it, lambda t: y_v[:, t * 128:(t + 1) * 128], *y_args)
        if it == 0:
            load_cols.wait()
            load_rows.wait()
            build(cols_v, spread_g)
            build(rows_v, spread_h)
            load_tiles.wait()
            for load in load_rest:
                load.wait()
        gather_wait(it, *y_args)
        products(it, y_full, rows_s, 0)
        grad = scatter_sum(it, spread_g, x_rows, g_send, g_recv, me_i, n_row, "row", gs_sem, gr_sem)
        bars = []
        for t in range(x_tiles):
            cut = slice(t * 128, (t + 1) * 128)
            x = x_v[:, cut]
            moved = x - PRIMAL_STEP * (cost_v[:, cut] - grad[t * 8:(t + 1) * 8])
            x_new = jnp.minimum(jnp.maximum(moved, 0.0), upper_v[:, cut])
            bars.append(2.0 * x_new - x)
            x_v[:, cut] = x_new
        x_args = (x_tiles, x_send, x_recv, x_full, me_i, n_row, "row", xs_sem, xr_sem)
        gather_start(it, lambda t: bars[t], *x_args)
        if last:
            store_x = pltpu.make_async_copy(x_v, out_x_h, out_sem.at[0])
            store_x.start()
        gather_wait(it, *x_args)
        products(it, x_full, cols_s, 1)
        image = scatter_sum(it, spread_h, y_rows, h_send, h_recv, me_j, n_col, "col", hs_sem, hr_sem)
        for t in range(y_tiles):
            cut = slice(t * 128, (t + 1) * 128)
            y_new = y_v[:, cut] + DUAL_STEP * (rhs_v[:, cut] - image[t * 8:(t + 1) * 8])
            y_v[:, cut] = jnp.where(kind_v[:, cut] == 1, jnp.maximum(y_new, 0.0), y_new)
    store_y = pltpu.make_async_copy(y_v, out_y_h, out_sem.at[1])
    store_y.start()
    for copy in sends:
        copy.wait_send()
    store_x.wait()
    store_y.wait()


def body(primal, dual, cost, upper, rhs, row_kind, tiles, tile_rows, tile_cols, tile_count):
    n_row = lax.axis_size("row")
    n_col = lax.axis_size("col")
    x_width, y_width = primal.shape[1], dual.shape[1]
    slots = tiles.shape[0]
    x_rows, y_rows = x_width // 16, y_width // 16
    g_rows, h_rows = x_rows * n_row, y_rows * n_col
    any_spec = pl.BlockSpec(memory_space=pl.ANY)
    smem_spec = pl.BlockSpec(memory_space=pltpu.SMEM)
    dma = pltpu.SemaphoreType.DMA
    scratch = [
        pltpu.VMEM((8, x_width), F32), pltpu.VMEM((8, y_width), F32), pltpu.VMEM((8, x_width), F32),
        pltpu.VMEM((1, x_width), F32), pltpu.VMEM((1, y_width), F32), pltpu.VMEM((1, y_width), jnp.int32),
        pltpu.VMEM(tiles.shape, BF16), pltpu.VMEM((1, slots), jnp.int32), pltpu.VMEM((1, slots), jnp.int32),
        pltpu.VMEM((g_rows, slots * 8), BF16), pltpu.VMEM((h_rows, slots * 8), BF16),
        pltpu.VMEM((slots * 8, 256), BF16),
        pltpu.VMEM((ITERS, y_rows, 128), BF16), pltpu.VMEM((ITERS, h_rows, 128), BF16),
        pltpu.VMEM((ITERS, h_rows // 8, 8, 128), F32),
        pltpu.VMEM((ITERS, x_rows, 128), BF16), pltpu.VMEM((ITERS, g_rows, 128), BF16),
        pltpu.VMEM((ITERS, g_rows // 8, 8, 128), F32),
        pltpu.VMEM((ITERS, n_row - 1, x_rows, 128), F32), pltpu.VMEM((ITERS, n_row - 1, x_rows, 128), F32),
        pltpu.VMEM((ITERS, n_col - 1, y_rows, 128), F32), pltpu.VMEM((ITERS, n_col - 1, y_rows, 128), F32),
        dma((9,)), dma((2,)),
        dma((ITERS, n_col - 1)), dma((ITERS, n_col - 1)), dma((ITERS, n_row - 1)), dma((ITERS, n_row - 1)),
        dma((ITERS, n_row - 1)), dma((ITERS, n_row - 1)), dma((ITERS, n_col - 1)), dma((ITERS, n_col - 1)),
    ]
    return pl.pallas_call(
        functools.partial(kernel, n_row, n_col),
        out_shape=(jax.ShapeDtypeStruct(primal.shape, F32), jax.ShapeDtypeStruct(dual.shape, F32)),
        in_specs=[any_spec] * 9 + [smem_spec] * 3,
        out_specs=(any_spec, any_spec),
        scratch_shapes=scratch,
        compiler_params=pltpu.CompilerParams(
            collective_id=0, has_side_effects=True, vmem_limit_bytes=40 * 1024 * 1024,
        ),
        name="pdhg",
    )(
        primal, dual, cost, upper.reshape(1, -1), rhs.reshape(1, -1), row_kind.reshape(1, -1), tiles,
        tile_rows.reshape(1, -1), tile_cols.reshape(1, -1), tile_count, tile_rows, tile_cols,
    )


def solution(mesh):
    in_specs = (
        P(None, ("col", "row")),
        P(None, ("row", "col")),
        P(None, ("col", "row")),
        P(("col", "row")),
        P(("row", "col")),
        P(("row", "col")),
        P(("row", "col"), None, None),
        P(("row", "col")),
        P(("row", "col")),
        P(("row", "col")),
    )
    out_specs = (P(None, ("col", "row")), P(None, ("row", "col")))
    return jax.shard_map(body, mesh=mesh, in_specs=in_specs, out_specs=out_specs, check_vma=False)
```

time: 180 us -> 53.2 us (0.30)
  waiting for transfers between devices: 103 us -> 0 us
  blocking collectives: 46.1 us -> 0 us
  Pallas kernels: 0 us -> 43.2 us
  between operations: 14.7 us -> 1.31 us
  other arithmetic: 5.77 us -> 0 us
  matrix products: 4.09 us -> 0 us
  local copies, waits for them, and re-layouts: 5.67 us -> 8.27 us
    reduce_scatter x4 -> x0, waiting for transfers between devices: 103 us -> none  [the longest x2 63.8 us: body(): lax.psum_scatter(partial_image, 'col', scatter_dimension=1, tiled=True)]
    all_gather x4 -> x0, blocking collectives: 46.1 us -> none  [the longest x2 26.2 us: body(): xbar_block = lax.all_gather(xbar, 'row', axis=1, tiled=True)]
    pallas_call x0 -> x1, Pallas kernels: none -> 43.2 us  [body(): pl.pallas_call(functools.partial(kernel, n_row, n_col), out_shape=(jax.Sh...]
    unnamed x24 -> x20, local copies, waits for them, and re-layouts: 3.24 us -> 8.27 us
    dot_general x8 -> x0, matrix products: 4.09 us -> none  [the longest x2 1.81 us: tile_forward(): jnp.einsum('rtk,tjk->rtj', pieces, tiles, preferred_element_type=jnp.floa...]
    convert_element_type x4 -> x0, other arithmetic: 3.69 us -> none  [the longest x2 2.16 us: body(): xbar = (2.0 * x_new - state_x).astype(jnp.bfloat16)]
    gather x4 -> x0, local copies, waits for them, and re-layouts: 2.43 us -> none  [the longest x2 1.22 us: tile_forward(): pieces = source.reshape(width, col_tiles, 128)[:, tile_cols]]
    select_n x3 -> x0, other arithmetic: 2.06 us -> none  [the longest x1 1.39 us: body(): y_new = jnp.where(kind_here[None, :] > 0.5, jnp.maximum(y_new, 0.0), y_new)]
  transfers between devices with their start and end apart: 4 -> 0, of which waited for: 4 -> 0; matrix products, arithmetic and copies ran while one was open for 0% -> 0% of each run, Pallas kernels for 0% -> 0%
where the time goes in v1:
time: 53.2 us; the launch traced here: 52.8 us
  Pallas kernels  43.2 us (81%)
  local copies, waits for them, and re-layouts  8.27 us (16%)
  between operations  1.31 us (2%)
    pallas_call x1, Pallas kernels, body(): pl.pallas_call(functools.partial(kernel, n_row, n_col), out_shape=(jax.Sh...  43.2 us
    unnamed x20, local copies, waits for them, and re-layouts  8.27 us

profile of v1, /device:TPU:0, one launch (start us, length us, event | category | flops | bytes accessed | tf_op | source)
XLA Modules:
  0.0 52.8 jit_solution(5219168619454381779)
XLA Ops:
  1.3 0.0 copy-start
  1.3 1.4 %copy-done = bf16[48,128,128]{2,1,0:T(8,128)(2,1)S(1)} copy-done((bf16[48,128,128]{2,1,0:T(8,128)(2,1)S(1)}, bf16[48,128,128]{2,1,0:T(8,128)(2,1)}, u32[]{:S(2)}) %copy-start) | copy-done | bytes 1572888
  2.7 0.0 copy-start.1
  2.7 0.8 %copy-done.1 = f32[8,1024]{1,0:T(8,128)S(1)} copy-done((f32[8,1024]{1,0:T(8,128)S(1)}, f32[8,1024]{1,0:T(8,128)}, u32[]{:S(2)}) %copy-start.1) | copy-done | bytes 32792
  3.4 0.0 copy-start.2
  3.4 0.8 %copy-done.2 = f32[8,1024]{1,0:T(8,128)S(1)} copy-done((f32[8,1024]{1,0:T(8,128)S(1)}, f32[8,1024]{1,0:T(8,128)}, u32[]{:S(2)}) %copy-start.2) | copy-done | bytes 32792
  4.2 0.0 copy-start.3
  4.2 0.8 %copy-done.3 = f32[8,1024]{1,0:T(8,128)S(1)} copy-done((f32[8,1024]{1,0:T(8,128)S(1)}, f32[8,1024]{1,0:T(8,128)}, u32[]{:S(2)}) %copy-start.3) | copy-done | bytes 32792
  5.0 0.0 copy-start.4
  5.0 0.7 %copy-done.4 = f32[1024]{0:T(1024)S(1)} copy-done((f32[1024]{0:T(1024)S(1)}, f32[1024]{0:T(1024)}, u32[]{:S(2)}) %copy-start.4) | copy-done | bytes 4120
  5.7 0.0 copy-start.5
  5.7 0.7 %copy-done.5 = f32[1024]{0:T(1024)S(1)} copy-done((f32[1024]{0:T(1024)S(1)}, f32[1024]{0:T(1024)}, u32[]{:S(2)}) %copy-start.5) | copy-done | bytes 4120
  6.3 0.0 copy-start.6
  6.3 0.7 %copy-done.6 = s32[1024]{0:T(1024)S(1)} copy-done((s32[1024]{0:T(1024)S(1)}, s32[1024]{0:T(1024)}, u32[]{:S(2)}) %copy-start.6) | copy-done | bytes 4120
  7.0 0.0 copy-start.7
  7.0 0.7 %copy-done.7 = s32[48]{0:T(128)S(1)} copy-done((s32[48]{0:T(128)S(1)}, s32[48]{0:T(128)}, u32[]{:S(2)}) %copy-start.7) | copy-done | bytes 216
  7.7 0.0 copy-start.8
  7.7 0.7 %copy-done.8 = s32[48]{0:T(128)S(1)} copy-done((s32[48]{0:T(128)S(1)}, s32[48]{0:T(128)}, u32[]{:S(2)}) %copy-start.8) | copy-done | bytes 216
  8.3 43.2 %pdhg.1 = (f32[8,1024]{1,0:T(8,128)S(1)}, f32[8,1024]{1,0:T(8,128)S(1)}) custom-call(f32[8,1024]{1,0:T(8,128)S(1)} %copy-done.1, f32[8,1024]{1,0:T(8,128)S(1)} %copy-done.2, f32[8,1024]{1,0:T(8,128)S(1)} %copy-done.3, f32[1,1024]{1,0:T(1,128)S(1)} %bitcast.5, f32[1,1024]{1,0:T(1,128)S(1)} %bitcast.6, s32[1,1024]{1,0:T(1,128)S(1)} %bitcast.7, ...), custom_call_target="tpu_custom_call" | custom-call | tf_op jit(solution)/shard_map/pdhg/pallas_call | solution.py:209
  51.5 0.6 %copy.15 = f32[8,1024]{1,0:T(8,128)} copy(f32[8,1024]{1,0:T(8,128)S(1)} %get-tuple-element.4) | data formatting | bytes 65536
  52.1 0.6 %copy.16 = f32[8,1024]{1,0:T(8,128)} copy(f32[8,1024]{1,0:T(8,128)S(1)} %get-tuple-element.5) | data formatting | bytes 65536
Async XLA Ops:
  1.3 1.4 %copy-start = (bf16[48,128,128]{2,1,0:T(8,128)(2,1)S(1)}, bf16[48,128,128]{2,1,0:T(8,128)(2,1)}, u32[]{:S(2)}) copy-start(bf16[48,128,128]{2,1,0:T(8,128)(2,1)} %tiles_h.1) | copy-start | bytes 4718596
  2.7 0.8 %copy-start.1 = (f32[8,1024]{1,0:T(8,128)S(1)}, f32[8,1024]{1,0:T(8,128)}, u32[]{:S(2)}) copy-start(f32[8,1024]{1,0:T(8,128)} %primal_h.1) | copy-start | bytes 98308
  3.4 0.8 %copy-start.2 = (f32[8,1024]{1,0:T(8,128)S(1)}, f32[8,1024]{1,0:T(8,128)}, u32[]{:S(2)}) copy-start(f32[8,1024]{1,0:T(8,128)} %dual_h.1) | copy-start | bytes 98308
  4.2 0.8 %copy-start.3 = (f32[8,1024]{1,0:T(8,128)S(1)}, f32[8,1024]{1,0:T(8,128)}, u32[]{:S(2)}) copy-start(f32[8,1024]{1,0:T(8,128)} %cost_h.1) | copy-start | bytes 98308
  5.0 0.7 %copy-start.4 = (f32[1024]{0:T(1024)S(1)}, f32[1024]{0:T(1024)}, u32[]{:S(2)}) copy-start(f32[1024]{0:T(1024)} %param.13) | copy-start | bytes 12292
  5.7 0.7 %copy-start.5 = (f32[1024]{0:T(1024)S(1)}, f32[1024]{0:T(1024)}, u32[]{:S(2)}) copy-start(f32[1024]{0:T(1024)} %param.14) | copy-start | bytes 12292
  6.3 0.7 %copy-start.6 = (s32[1024]{0:T(1024)S(1)}, s32[1024]{0:T(1024)}, u32[]{:S(2)}) copy-start(s32[1024]{0:T(1024)} %param.15) | copy-start | bytes 12292
  7.0 0.7 %copy-start.7 = (s32[48]{0:T(128)S(1)}, s32[48]{0:T(128)}, u32[]{:S(2)}) copy-start(s32[48]{0:T(128)} %rows_s.1) | copy-start | bytes 580
  7.7 0.7 %copy-start.8 = (s32[48]{0:T(128)S(1)}, s32[48]{0:T(128)}, u32[]{:S(2)}) copy-start(s32[48]{0:T(128)} %cols_s.1) | copy-start | bytes 580

commit v2 on v1

--- a/solution.py
+++ b/solution.py
@@ -97,22 +97,22 @@
             contrib[s * 8:(s + 2) * 8, :128] = high
             contrib[s * 8:(s + 2) * 8, 128:] = (both - high.astype(F32)).astype(BF16)
 
-    def spread(matrix, block, rows):
-        part = matrix[pl.ds(pl.multiple_of(block * rows, 16), rows), :]
-        total = jnp.dot(part, contrib[...], preferred_element_type=F32)
-        return total[:, :128] + total[:, 128:]
-
     def scatter_sum(it, matrix, rows, send, recv, me, n, axis, s_sem, r_sem):
+        whole = jnp.dot(matrix[...], contrib[...], preferred_element_type=F32)
+        send[it] = whole[:, :128] + whole[:, 128:]
+
+        def block(index):
+            return send.at[it, pl.ds(pl.multiple_of(index * rows, 16), rows), :]
+
         for d in range(1, n):
             target = lax.rem(me + d, n)
-            send[it, d - 1] = spread(matrix, target, rows)
-            push(send.at[it, d - 1], recv.at[it, d - 1], s_sem.at[it, d - 1], r_sem.at[it, d - 1], {axis: target})
-        total = spread(matrix, me, rows)
-        for d in range(1, n):
+            push(block(target), recv.at[it, d - 1], s_sem.at[it, d - 1], r_sem.at[it, d - 1], {axis: target})
+        total = block(me)[...]
+        for d in range(1, n):
+            source = lax.rem(me + n - d, n)
             pltpu.make_async_remote_copy(
-                src_ref=send.at[it, d - 1], dst_ref=recv.at[it, d - 1], send_sem=s_sem.at[it, d - 1],
-                recv_sem=r_sem.at[it, d - 1], device_id={axis: lax.rem(me + d, n)},
-                device_id_type=pl.DeviceIdType.MESH,
+                src_ref=block(source), dst_ref=recv.at[it, d - 1], send_sem=s_sem.at[it, d - 1],
+                recv_sem=r_sem.at[it, d - 1], device_id={axis: source}, device_id_type=pl.DeviceIdType.MESH,
             ).wait_recv()
             total = total + recv[it, d - 1]
         return total
@@ -200,8 +200,8 @@
         pltpu.VMEM((ITERS, h_rows // 8, 8, 128), F32),
         pltpu.VMEM((ITERS, x_rows, 128), BF16), pltpu.VMEM((ITERS, g_rows, 128), BF16),
         pltpu.VMEM((ITERS, g_rows // 8, 8, 128), F32),
-        pltpu.VMEM((ITERS, n_row - 1, x_rows, 128), F32), pltpu.VMEM((ITERS, n_row - 1, x_rows, 128), F32),
-        pltpu.VMEM((ITERS, n_col - 1, y_rows, 128), F32), pltpu.VMEM((ITERS, n_col - 1, y_rows, 128), F32),
+        pltpu.VMEM((ITERS, g_rows, 128), F32), pltpu.VMEM((ITERS, n_row - 1, x_rows, 128), F32),
+        pltpu.VMEM((ITERS, h_rows, 128), F32), pltpu.VMEM((ITERS, n_col - 1, y_rows, 128), F32),
         dma((9,)), dma((2,)),
         dma((ITERS, n_col - 1)), dma((ITERS, n_col - 1)), dma((ITERS, n_row - 1)), dma((ITERS, n_row - 1)),
         dma((ITERS, n_row - 1)), dma((ITERS, n_row - 1)), dma((ITERS, n_col - 1)), dma((ITERS, n_col - 1)),
@@ -213,7 +213,7 @@
         out_specs=(any_spec, any_spec),
         scratch_shapes=scratch,
         compiler_params=pltpu.CompilerParams(
-            collective_id=0, has_side_effects=True, vmem_limit_bytes=40 * 1024 * 1024,
+            collective_id=0, has_side_effects=True, vmem_limit_bytes=60 * 1024 * 1024,
         ),
         name="pdhg",
     )(

time: 53.2 us -> 48.1 us (0.904)
  local copies, waits for them, and re-layouts: 8.27 us -> 2.75 us
  Pallas kernels: 43.2 us -> 43.8 us
    unnamed x20 -> x2, local copies, waits for them, and re-layouts: 8.27 us -> 2.75 us
    pallas_call x1, Pallas kernels: 43.2 us -> 43.8 us  [body(): pl.pallas_call(functools.partial(kernel, n_row, n_col), out_shape=(jax.Sh...]
where the time goes in v2:
time: 48.1 us; the launch traced here: 47.8 us
  Pallas kernels  43.8 us (91%)
  local copies, waits for them, and re-layouts  2.75 us (6%)
  between operations  1.29 us (3%)
    pallas_call x1, Pallas kernels, body(): pl.pallas_call(functools.partial(kernel, n_row, n_col), out_shape=(jax.Sh...  43.8 us
    unnamed x2, local copies, waits for them, and re-layouts  2.75 us

profile of v2, /device:TPU:0, one launch (start us, length us, event | category | flops | bytes accessed | tf_op | source)
XLA Modules:
  0.0 47.8 jit_solution(6831422005187818761)
XLA Ops:
  1.3 43.8 %pdhg.1 = (f32[8,1024]{1,0:T(8,128)}, f32[8,1024]{1,0:T(8,128)}) custom-call(f32[8,1024]{1,0:T(8,128)} %primal_h.1, f32[8,1024]{1,0:T(8,128)} %dual_h.1, f32[8,1024]{1,0:T(8,128)} %cost_h.1, f32[1,1024]{1,0:T(1,128)} %bitcast.5, f32[1,1024]{1,0:T(1,128)} %bitcast.6, s32[1,1024]{1,0:T(1,128)} %bitcast.7, bf16[48,128,128]{2,1,0:T(8,128)(2,1)} %tiles_h.1, ...), custom_call_target="tpu_custom_call" | custom-call | tf_op jit(solution)/shard_map/pdhg/pallas_call | solution.py:209
  45.0 1.4 %copy.15 = f32[8,1024]{1,0:T(8,128)} copy(f32[8,1024]{1,0:T(8,128)} %get-tuple-element.4) | data formatting | bytes 65536
  46.4 1.4 %copy.16 = f32[8,1024]{1,0:T(8,128)} copy(f32[8,1024]{1,0:T(8,128)} %get-tuple-element.5) | data formatting | bytes 65536

commit v3 on v2

v3 whole, which is shorter than its diff:
```python
import functools

import jax
import jax.numpy as jnp
from jax import lax
from jax.experimental import pallas as pl
from jax.experimental.pallas import tpu as pltpu
from jax.sharding import PartitionSpec as P

ITERS = 2
GROUPS = 2
HALF = 4
PRIMAL_STEP = 0.4
DUAL_STEP = 0.4
BF16 = jnp.bfloat16
F32 = jnp.float32


def kernel(
    n_row, n_col,
    primal_h, dual_h, cost_h, upper_h, rhs_h, kind_h, tiles_h, rows_h, cols_h, count_s, rows_s, cols_s,
    out_x_h, out_y_h,
    x_v, y_v, cost_v, upper_v, rhs_v, kind_v, tiles_v, rows_v, cols_v,
    x_st, y_st, cost_st, upper_st, rhs_st, kind_st,
    spread_g, spread_h, contrib,
    y_send, y_recv, y_full, x_send, x_recv, x_full,
    g_send, g_recv, h_send, h_recv,
    in_sem, out_sem, ys_sem, yr_sem, gs_sem, gr_sem, xs_sem, xr_sem, hs_sem, hr_sem,
):
    me_i = lax.axis_index("row")
    me_j = lax.axis_index("col")
    slots = tiles_v.shape[0]
    x_tiles = x_v.shape[1] // 128
    y_tiles = y_v.shape[1] // 128

    barrier = pltpu.get_barrier_semaphore()
    for d in range(1, n_col):
        pl.semaphore_signal(barrier, inc=1, device_id={"col": lax.rem(me_j + d, n_col)}, device_id_type=pl.DeviceIdType.MESH)
    for d in range(1, n_row):
        pl.semaphore_signal(barrier, inc=1, device_id={"row": lax.rem(me_i + d, n_row)}, device_id_type=pl.DeviceIdType.MESH)

    loads = [
        pltpu.make_async_copy(src, dst, in_sem.at[k])
        for k, (src, dst) in enumerate((
            (dual_h, y_v), (cols_h, cols_v), (rows_h, rows_v), (tiles_h, tiles_v), (primal_h, x_v),
            (cost_h, cost_v), (upper_h, upper_v), (rhs_h, rhs_v), (kind_h, kind_v),
        ))
    ]
    for load in loads:
        load.start()

    def to_rows(ref, group, tiles):
        return jnp.concatenate(
            [ref[group * HALF:(group + 1) * HALF, t * 128:(t + 1) * 128] for t in range(tiles)], axis=0
        )

    def spread_rows(ref, tiles):
        return jnp.concatenate(
            [jnp.broadcast_to(ref[:, t * 128:(t + 1) * 128], (HALF, 128)) for t in range(tiles)], axis=0
        )

    def from_rows(ref, group, value, tiles):
        for t in range(tiles):
            ref[group * HALF:(group + 1) * HALF, t * 128:(t + 1) * 128] = value[t * HALF:(t + 1) * HALF]

    def push(src, dst, send_sem, recv_sem, device):
        pltpu.make_async_remote_copy(
            src_ref=src, dst_ref=dst, send_sem=send_sem, recv_sem=recv_sem,
            device_id=device, device_id_type=pl.DeviceIdType.MESH,
        ).start()

    def drain(recv, sem, it, group):
        whole = recv.at[it, group]
        pltpu.make_async_copy(whole, whole, sem.at[it, group]).wait()

    def fill(full, it, group, first, value, tiles):
        for t in range(tiles):
            part = value[t * HALF:(t + 1) * HALF]
            full[it, group, first + t] = jnp.concatenate([part, part], axis=0)

    def gather_start(it, group, value, tiles, send, recv, full, me, n, axis, s_sem, r_sem):
        low = value.astype(BF16)
        send[it, group] = low
        for d in range(1, n):
            push(
                send.at[it, group], recv.at[it, group, d - 1], s_sem.at[it, group], r_sem.at[it, group],
                {axis: lax.rem(me + d, n)},
            )
        fill(full, it, group, me * tiles, low.astype(F32), tiles)

    def gather_wait(it, group, tiles, send, recv, full, me, n, axis, s_sem, r_sem):
        drain(recv, r_sem, it, group)
        for d in range(1, n):
            source = lax.rem(me + n - d, n)
            fill(full, it, group, source * tiles, recv[it, group, d - 1].astype(F32), tiles)

    upper_half = lax.broadcasted_iota(jnp.int32, (8, 128), 0) < HALF

    def products(it, group, full, index, forward):
        for s in range(0, slots, 2):
            one = jnp.where(upper_half, full[it, group, index[s]], 0.0)
            two = jnp.where(upper_half, 0.0, full[it, group, index[s + 1]])
            left = jnp.concatenate([one, two], axis=1).astype(BF16)
            if forward:
                right = jnp.concatenate([tiles_v[s], tiles_v[s + 1]], axis=1)
                both = lax.dot_general(left, right, (((1,), (1,)), ((), ())), preferred_element_type=F32)
            else:
                right = tiles_v[s:s + 2].reshape(256, 128)
                both = jnp.dot(left, right, preferred_element_type=F32)
            contrib[group, s * HALF:(s + 2) * HALF, :] = both

    def scatter_start(it, group, matrix, rows, send, recv, me, n, axis, s_sem, r_sem):
        terms = contrib[group]
        high = terms.astype(BF16)
        rest = (terms - high.astype(F32)).astype(BF16)
        whole = jnp.dot(matrix[...], jnp.concatenate([high, rest], axis=1), preferred_element_type=F32)
        send[it, group] = (whole[:, :128] + whole[:, 128:]).reshape(n, rows, 128)
        for d in range(1, n):
            target = lax.rem(me + d, n)
            push(
                send.at[it, group, target], recv.at[it, group, d - 1], s_sem.at[it, group], r_sem.at[it, group],
                {axis: target},
            )

    def scatter_wait(it, group, matrix, rows, send, recv, me, n, axis, s_sem, r_sem):
        drain(recv, r_sem, it, group)
        total = send[it, group, me]
        for d in range(1, n):
            total = total + recv[it, group, d - 1]
        return total

    lanes = slots * HALF

    def build(index_v, matrix):
        slot = lax.broadcasted_iota(jnp.int32, (8, slots), 1)
        place = jnp.where(slot < count_s[0], jnp.broadcast_to(index_v[...], (8, slots)), -1)
        lane = lax.broadcasted_iota(jnp.int32, (slots, lanes), 1)
        wider = (lane // HALF == lax.broadcasted_iota(jnp.int32, (slots, lanes), 0)).astype(F32).astype(BF16)
        place = jnp.dot(place.astype(F32).astype(BF16), wider, preferred_element_type=F32)
        sub = lax.broadcasted_iota(jnp.int32, (8, lanes), 0)
        own = lax.broadcasted_iota(jnp.int32, (8, lanes), 1) % HALF == sub % HALF
        place = jnp.where(own, place, -100000.0).astype(jnp.int32) - sub // HALF
        two = jnp.concatenate([place, place - 2], axis=0)

        def step(c, carry):
            matrix[pl.ds(pl.multiple_of(c * 16, 16), 16), :] = jnp.where(two == 4 * c, 1.0, 0.0).astype(BF16)
            return carry

        lax.fori_loop(0, matrix.shape[0] // 16, step, 0)

    y_args = (y_tiles, y_send, y_recv, y_full, me_j, n_col, "col", ys_sem, yr_sem)
    x_args = (x_tiles, x_send, x_recv, x_full, me_i, n_row, "row", xs_sem, xr_sem)
    g_args = (spread_g, x_tiles * HALF, g_send, g_recv, me_i, n_row, "row", gs_sem, gr_sem)
    h_args = (spread_h, y_tiles * HALF, h_send, h_recv, me_j, n_col, "col", hs_sem, hr_sem)

    loads[0].wait()
    for group in range(GROUPS):
        y_st[group] = to_rows(y_v, group, y_tiles)
    pl.semaphore_wait(barrier, n_row + n_col - 2)
    for group in range(GROUPS):
        gather_start(0, group, y_st[group], *y_args)
    for load in loads[1:]:
        load.wait()
    build(cols_v, spread_g)
    build(rows_v, spread_h)
    for group in range(GROUPS):
        x_st[group] = to_rows(x_v, group, x_tiles)
        cost_st[group] = to_rows(cost_v, group, x_tiles)
    upper_st[...] = spread_rows(upper_v, x_tiles)
    rhs_st[...] = spread_rows(rhs_v, y_tiles)
    kind_st[...] = spread_rows(kind_v, y_tiles)
    stores = (pltpu.make_async_copy(x_v, out_x_h, out_sem.at[0]), pltpu.make_async_copy(y_v, out_y_h, out_sem.at[1]))
    for it in range(ITERS):
        last = it == ITERS - 1
        for group in range(GROUPS):
            gather_wait(it, group, *y_args)
            products(it, group, y_full, rows_s, False)
            scatter_start(it, group, *g_args)
        for group in range(GROUPS):
            grad = scatter_wait(it, group, *g_args)
            x = x_st[group]
            moved = x - PRIMAL_STEP * (cost_st[group] - grad)
            x_new = jnp.minimum(jnp.maximum(moved, 0.0), upper_st[...])
            gather_start(it, group, 2.0 * x_new - x, *x_args)
            x_st[group] = x_new
            if last:
                from_rows(x_v, group, x_new, x_tiles)
        if last:
            stores[0].start()
        for group in range(GROUPS):
            gather_wait(it, group, *x_args)
            products(it, group, x_full, cols_s, True)
            scatter_start(it, group, *h_args)
        for group in range(GROUPS):
            image = scatter_wait(it, group, *h_args)
            y_new = y_st[group] + DUAL_STEP * (rhs_st[...] - image)
            y_new = jnp.where(kind_st[...] == 1, jnp.maximum(y_new, 0.0), y_new)
            if last:
                from_rows(y_v, group, y_new, y_tiles)
            else:
                y_st[group] = y_new
                gather_start(it + 1, group, y_new, *y_args)
    stores[1].start()
    for it in range(ITERS):
        for group in range(GROUPS):
            drain(y_recv, ys_sem, it, group)
            drain(g_recv, gs_sem, it, group)
            drain(x_recv, xs_sem, it, group)
            drain(h_recv, hs_sem, it, group)
    for store in stores:
        store.wait()


def hand_out(x_in, y_in, x_out, y_out, sem):
    copies = (pltpu.make_async_copy(x_in, x_out, sem.at[0]), pltpu.make_async_copy(y_in, y_out, sem.at[1]))
    for copy in copies:
        copy.start()
    for copy in copies:
        copy.wait()


def body(primal, dual, cost, upper, rhs, row_kind, tiles, tile_rows, tile_cols, tile_count):
    n_row = lax.axis_size("row")
    n_col = lax.axis_size("col")
    x_width, y_width = primal.shape[1], dual.shape[1]
    slots = tiles.shape[0]
    x_rows, y_rows = x_width // 128 * HALF, y_width // 128 * HALF
    any_spec = pl.BlockSpec(memory_space=pl.ANY)
    smem_spec = pl.BlockSpec(memory_space=pltpu.SMEM)
    dma = pltpu.SemaphoreType.DMA
    both = (ITERS, GROUPS)

    def exchange(n, rows):
        return [
            pltpu.VMEM(both + (rows, 128), BF16), pltpu.VMEM(both + (n - 1, rows, 128), BF16),
            pltpu.VMEM(both + (n * rows // HALF, 8, 128), F32),
        ]

    def partial(n, rows):
        return [pltpu.VMEM(both + (n, rows, 128), F32), pltpu.VMEM(both + (n - 1, rows, 128), F32)]

    scratch = [
        pltpu.VMEM((8, x_width), F32), pltpu.VMEM((8, y_width), F32), pltpu.VMEM((8, x_width), F32),
        pltpu.VMEM((1, x_width), F32), pltpu.VMEM((1, y_width), F32), pltpu.VMEM((1, y_width), jnp.int32),
        pltpu.VMEM(tiles.shape, BF16), pltpu.VMEM((1, slots), jnp.int32), pltpu.VMEM((1, slots), jnp.int32),
        pltpu.VMEM((GROUPS, x_rows, 128), F32), pltpu.VMEM((GROUPS, y_rows, 128), F32),
        pltpu.VMEM((GROUPS, x_rows, 128), F32), pltpu.VMEM((x_rows, 128), F32),
        pltpu.VMEM((y_rows, 128), F32), pltpu.VMEM((y_rows, 128), jnp.int32),
        pltpu.VMEM((x_rows * n_row, slots * HALF), BF16), pltpu.VMEM((y_rows * n_col, slots * HALF), BF16),
        pltpu.VMEM((GROUPS, slots * HALF, 128), F32),
    ]
    scratch += exchange(n_col, y_rows) + exchange(n_row, x_rows) + partial(n_row, x_rows) + partial(n_col, y_rows)
    scratch += [dma((9,)), dma((2,))] + [dma(both)] * 8
    results = pl.pallas_call(
        functools.partial(kernel, n_row, n_col),
        out_shape=(jax.ShapeDtypeStruct(primal.shape, F32), jax.ShapeDtypeStruct(dual.shape, F32)),
        in_specs=[any_spec] * 9 + [smem_spec] * 3,
        out_specs=(any_spec, any_spec),
        scratch_shapes=scratch,
        compiler_params=pltpu.CompilerParams(
            collective_id=0, has_side_effects=True, vmem_limit_bytes=60 * 1024 * 1024,
        ),
        name="pdhg",
    )(
        primal, dual, cost, upper.reshape(1, -1), rhs.reshape(1, -1), row_kind.reshape(1, -1), tiles,
        tile_rows.reshape(1, -1), tile_cols.reshape(1, -1), tile_count, tile_rows, tile_cols,
    )
    return pl.pallas_call(
        hand_out,
        out_shape=(jax.ShapeDtypeStruct(primal.shape, F32), jax.ShapeDtypeStruct(dual.shape, F32)),
        in_specs=[any_spec] * 2,
        out_specs=(any_spec, any_spec),
        scratch_shapes=[dma((2,))],
        compiler_params=pltpu.CompilerParams(vmem_limit_bytes=60 * 1024 * 1024),
        name="hand_out",
    )(*results)


def solution(mesh):
    in_specs = (
        P(None, ("col", "row")),
        P(None, ("row", "col")),
        P(None, ("col", "row")),
        P(("col", "row")),
        P(("row", "col")),
        P(("row", "col")),
        P(("row", "col"), None, None),
        P(("row", "col")),
        P(("row", "col")),
        P(("row", "col")),
    )
    out_specs = (P(None, ("col", "row")), P(None, ("row", "col")))
    return jax.shard_map(body, mesh=mesh, in_specs=in_specs, out_specs=out_specs, check_vma=False)
```

time: 48.1 us -> 44.2 us (0.919)
  local copies, waits for them, and re-layouts: 2.75 us -> 0 us
  Pallas kernels: 43.8 us -> 42.7 us
    pallas_call x1, Pallas kernels: 43.8 us -> 39.6 us  [body(): pl.pallas_call(functools.partial(kernel, n_row, n_col), out_shape=(jax.Sh...]
    pallas_call x0 -> x1, Pallas kernels: none -> 3.11 us  [body(): pl.pallas_call(hand_out, out_shape=(jax.ShapeDtypeStruct(primal.shape, F3...]
    unnamed x2 -> x0, local copies, waits for them, and re-layouts: 2.75 us -> none
where the time goes in v3:
time: 44.2 us; the launch traced here: 44 us
  Pallas kernels  42.7 us (97%)
  between operations  1.29 us (3%)
    pallas_call x1, Pallas kernels, body(): pl.pallas_call(functools.partial(kernel, n_row, n_col), out_shape=(jax.Sh...  39.6 us
    pallas_call x1, Pallas kernels, body(): pl.pallas_call(hand_out, out_shape=(jax.ShapeDtypeStruct(primal.shape, F3...  3.11 us

profile of v3, /device:TPU:0, one launch (start us, length us, event | category | flops | bytes accessed | tf_op | source)
XLA Modules:
  0.0 44.0 jit_solution(6826763007696693325)
XLA Ops:
  1.3 39.6 %pdhg.1 = (f32[8,1024]{1,0:T(8,128)}, f32[8,1024]{1,0:T(8,128)}) custom-call(f32[8,1024]{1,0:T(8,128)} %primal_h.1, f32[8,1024]{1,0:T(8,128)} %dual_h.1, f32[8,1024]{1,0:T(8,128)} %cost_h.1, f32[1,1024]{1,0:T(1,128)} %bitcast.5, f32[1,1024]{1,0:T(1,128)} %bitcast.6, s32[1,1024]{1,0:T(1,128)} %bitcast.7, bf16[48,128,128]{2,1,0:T(8,128)(2,1)} %tiles_h.1, ...), custom_call_target="tpu_custom_call" | custom-call | tf_op jit(solution)/shard_map/pdhg/pallas_call | solution.py:254
  40.9 3.1 %hand_out.1 = (f32[8,1024]{1,0:T(8,128)}, f32[8,1024]{1,0:T(8,128)}) custom-call(f32[8,1024]{1,0:T(8,128)} %get-tuple-element.4.x_in, f32[8,1024]{1,0:T(8,128)} %get-tuple-element.5.y_in), custom_call_target="tpu_custom_call" | custom-call | tf_op jit(solution)/shard_map/hand_out/pallas_call | solution.py:268

commit v4 on v3

--- a/solution.py
+++ b/solution.py
@@ -18,13 +18,13 @@
 
 def kernel(
     n_row, n_col,
-    primal_h, dual_h, cost_h, upper_h, rhs_h, kind_h, tiles_h, rows_h, cols_h, count_s, rows_s, cols_s,
+    primal_h, dual_h, cost_h, upper_h, rhs_h, kind_h, tiles_h, rows_h, cols_h, count_s,
     out_x_h, out_y_h,
-    x_v, y_v, cost_v, upper_v, rhs_v, kind_v, tiles_v, rows_v, cols_v,
+    x_v, y_v, cost_v, upper_v, rhs_v, kind_v, tiles_v, rows_v, cols_v, rows_s, cols_s,
     x_st, y_st, cost_st, upper_st, rhs_st, kind_st,
-    spread_g, spread_h, contrib,
+    turned, spread_g, spread_h, contrib,
     y_send, y_recv, y_full, x_send, x_recv, x_full,
-    g_send, g_recv, h_send, h_recv,
+    g_send, g_recv, h_send, h_recv, low_send, low_recv,
     in_sem, out_sem, ys_sem, yr_sem, gs_sem, gr_sem, xs_sem, xr_sem, hs_sem, hr_sem,
 ):
     me_i = lax.axis_index("row")
@@ -44,6 +44,7 @@
         for k, (src, dst) in enumerate((
             (dual_h, y_v), (cols_h, cols_v), (rows_h, rows_v), (tiles_h, tiles_v), (primal_h, x_v),
             (cost_h, cost_v), (upper_h, upper_v), (rhs_h, rhs_v), (kind_h, kind_v),
+            (rows_h, rows_s), (cols_h, cols_s),
         ))
     ]
     for load in loads:
@@ -71,6 +72,10 @@
 
     def drain(recv, sem, it, group):
         whole = recv.at[it, group]
+        pltpu.make_async_copy(whole, whole, sem.at[it, group]).wait()
+
+    def drain_low(sem, it, group):
+        whole = low_recv.at[group]
         pltpu.make_async_copy(whole, whole, sem.at[it, group]).wait()
 
     def fill(full, it, group, first, value, tiles):
@@ -96,37 +101,43 @@
 
     upper_half = lax.broadcasted_iota(jnp.int32, (8, 128), 0) < HALF
 
-    def products(it, group, full, index, forward):
+    def products(it, group, full, index, blocks):
         for s in range(0, slots, 2):
-            one = jnp.where(upper_half, full[it, group, index[s]], 0.0)
-            two = jnp.where(upper_half, 0.0, full[it, group, index[s + 1]])
+            one = jnp.where(upper_half, full[it, group, index[0, s]], 0.0)
+            two = jnp.where(upper_half, 0.0, full[it, group, index[0, s + 1]])
             left = jnp.concatenate([one, two], axis=1).astype(BF16)
-            if forward:
-                right = jnp.concatenate([tiles_v[s], tiles_v[s + 1]], axis=1)
-                both = lax.dot_general(left, right, (((1,), (1,)), ((), ())), preferred_element_type=F32)
-            else:
-                right = tiles_v[s:s + 2].reshape(256, 128)
-                both = jnp.dot(left, right, preferred_element_type=F32)
+            both = jnp.dot(left, blocks[s:s + 2].reshape(256, 128), preferred_element_type=F32)
             contrib[group, s * HALF:(s + 2) * HALF, :] = both
 
-    def scatter_start(it, group, matrix, rows, send, recv, me, n, axis, s_sem, r_sem):
+    def scatter_start(it, group, matrix, rows, send, recv, me, n, axis, s_sem, r_sem, narrow=False):
         terms = contrib[group]
         high = terms.astype(BF16)
         rest = (terms - high.astype(F32)).astype(BF16)
         whole = jnp.dot(matrix[...], jnp.concatenate([high, rest], axis=1), preferred_element_type=F32)
         send[it, group] = (whole[:, :128] + whole[:, 128:]).reshape(n, rows, 128)
+        if narrow:
+            low_send[group] = send[it, group].astype(BF16)
         for d in range(1, n):
             target = lax.rem(me + d, n)
+            if narrow:
+                push(
+                    low_send.at[group, target], low_recv.at[group, d - 1], s_sem.at[it, group], r_sem.at[it, group],
+                    {axis: target},
+                )
+                continue
             push(
                 send.at[it, group, target], recv.at[it, group, d - 1], s_sem.at[it, group], r_sem.at[it, group],
                 {axis: target},
             )
 
-    def scatter_wait(it, group, matrix, rows, send, recv, me, n, axis, s_sem, r_sem):
-        drain(recv, r_sem, it, group)
+    def scatter_wait(it, group, matrix, rows, send, recv, me, n, axis, s_sem, r_sem, narrow=False):
         total = send[it, group, me]
+        if narrow:
+            drain_low(r_sem, it, group)
+        else:
+            drain(recv, r_sem, it, group)
         for d in range(1, n):
-            total = total + recv[it, group, d - 1]
+            total = total + (low_recv[group, d - 1].astype(F32) if narrow else recv[it, group, d - 1])
         return total
 
     lanes = slots * HALF
@@ -162,7 +173,6 @@
     for load in loads[1:]:
         load.wait()
     build(cols_v, spread_g)
-    build(rows_v, spread_h)
     for group in range(GROUPS):
         x_st[group] = to_rows(x_v, group, x_tiles)
         cost_st[group] = to_rows(cost_v, group, x_tiles)
@@ -174,8 +184,12 @@
         last = it == ITERS - 1
         for group in range(GROUPS):
             gather_wait(it, group, *y_args)
-            products(it, group, y_full, rows_s, False)
+            products(it, group, y_full, rows_s, tiles_v)
             scatter_start(it, group, *g_args)
+        if it == 0:
+            for s in range(slots):
+                turned[s] = tiles_v[s].T
+            build(rows_v, spread_h)
         for group in range(GROUPS):
             grad = scatter_wait(it, group, *g_args)
             x = x_st[group]
@@ -189,10 +203,10 @@
             stores[0].start()
         for group in range(GROUPS):
             gather_wait(it, group, *x_args)
-            products(it, group, x_full, cols_s, True)
-            scatter_start(it, group, *h_args)
-        for group in range(GROUPS):
-            image = scatter_wait(it, group, *h_args)
+            products(it, group, x_full, cols_s, turned)
+            scatter_start(it, group, *h_args, narrow=last)
+        for group in range(GROUPS):
+            image = scatter_wait(it, group, *h_args, narrow=last)
             y_new = y_st[group] + DUAL_STEP * (rhs_st[...] - image)
             y_new = jnp.where(kind_st[...] == 1, jnp.maximum(y_new, 0.0), y_new)
             if last:
@@ -206,17 +220,12 @@
             drain(y_recv, ys_sem, it, group)
             drain(g_recv, gs_sem, it, group)
             drain(x_recv, xs_sem, it, group)
-            drain(h_recv, hs_sem, it, group)
+            if it == ITERS - 1:
+                drain_low(hs_sem, it, group)
+            else:
+                drain(h_recv, hs_sem, it, group)
     for store in stores:
         store.wait()
-
-
-def hand_out(x_in, y_in, x_out, y_out, sem):
-    copies = (pltpu.make_async_copy(x_in, x_out, sem.at[0]), pltpu.make_async_copy(y_in, y_out, sem.at[1]))
-    for copy in copies:
-        copy.start()
-    for copy in copies:
-        copy.wait()
 
 
 def body(primal, dual, cost, upper, rhs, row_kind, tiles, tile_rows, tile_cols, tile_count):
@@ -226,7 +235,6 @@
     slots = tiles.shape[0]
     x_rows, y_rows = x_width // 128 * HALF, y_width // 128 * HALF
     any_spec = pl.BlockSpec(memory_space=pl.ANY)
-    smem_spec = pl.BlockSpec(memory_space=pltpu.SMEM)
     dma = pltpu.SemaphoreType.DMA
     both = (ITERS, GROUPS)
 
@@ -243,37 +251,37 @@
         pltpu.VMEM((8, x_width), F32), pltpu.VMEM((8, y_width), F32), pltpu.VMEM((8, x_width), F32),
         pltpu.VMEM((1, x_width), F32), pltpu.VMEM((1, y_width), F32), pltpu.VMEM((1, y_width), jnp.int32),
         pltpu.VMEM(tiles.shape, BF16), pltpu.VMEM((1, slots), jnp.int32), pltpu.VMEM((1, slots), jnp.int32),
+        pltpu.SMEM((1, slots), jnp.int32), pltpu.SMEM((1, slots), jnp.int32),
         pltpu.VMEM((GROUPS, x_rows, 128), F32), pltpu.VMEM((GROUPS, y_rows, 128), F32),
         pltpu.VMEM((GROUPS, x_rows, 128), F32), pltpu.VMEM((x_rows, 128), F32),
         pltpu.VMEM((y_rows, 128), F32), pltpu.VMEM((y_rows, 128), jnp.int32),
+        pltpu.VMEM(tiles.shape, BF16),
         pltpu.VMEM((x_rows * n_row, slots * HALF), BF16), pltpu.VMEM((y_rows * n_col, slots * HALF), BF16),
         pltpu.VMEM((GROUPS, slots * HALF, 128), F32),
     ]
     scratch += exchange(n_col, y_rows) + exchange(n_row, x_rows) + partial(n_row, x_rows) + partial(n_col, y_rows)
-    scratch += [dma((9,)), dma((2,))] + [dma(both)] * 8
-    results = pl.pallas_call(
+    scratch += [pltpu.VMEM((GROUPS, n_col, y_rows, 128), BF16), pltpu.VMEM((GROUPS, n_col - 1, y_rows, 128), BF16)]
+    scratch += [dma((11,)), dma((2,))] + [dma(both)] * 8
+    operands = [
+        pltpu.with_memory_space_constraint(operand, pltpu.HBM)
+        for operand in (
+            primal, dual, cost, upper.reshape(1, -1), rhs.reshape(1, -1), row_kind.reshape(1, -1), tiles,
+            tile_rows.reshape(1, -1), tile_cols.reshape(1, -1),
+        )
+    ]
+    return pl.pallas_call(
         functools.partial(kernel, n_row, n_col),
         out_shape=(jax.ShapeDtypeStruct(primal.shape, F32), jax.ShapeDtypeStruct(dual.shape, F32)),
-        in_specs=[any_spec] * 9 + [smem_spec] * 3,
+        in_specs=[any_spec] * 9 + [pl.BlockSpec(memory_space=pltpu.SMEM)],
         out_specs=(any_spec, any_spec),
         scratch_shapes=scratch,
         compiler_params=pltpu.CompilerParams(
-            collective_id=0, has_side_effects=True, vmem_limit_bytes=60 * 1024 * 1024,
+            collective_id=0, has_side_effects=True, vmem_limit_bytes=40 * 1024 * 1024,
         ),
         name="pdhg",
     )(
-        primal, dual, cost, upper.reshape(1, -1), rhs.reshape(1, -1), row_kind.reshape(1, -1), tiles,
-        tile_rows.reshape(1, -1), tile_cols.reshape(1, -1), tile_count, tile_rows, tile_cols,
+        *operands, tile_count,
     )
-    return pl.pallas_call(
-        hand_out,
-        out_shape=(jax.ShapeDtypeStruct(primal.shape, F32), jax.ShapeDtypeStruct(dual.shape, F32)),
-        in_specs=[any_spec] * 2,
-        out_specs=(any_spec, any_spec),
-        scratch_shapes=[dma((2,))],
-        compiler_params=pltpu.CompilerParams(vmem_limit_bytes=60 * 1024 * 1024),
-        name="hand_out",
-    )(*results)
 
 
 def solution(mesh):

time: 44.2 us -> 40.5 us (0.916)
  Pallas kernels: 42.7 us -> 37.8 us
  local copies, waits for them, and re-layouts: 0 us -> 1.23 us
    pallas_call x1 -> x0, Pallas kernels: 3.11 us -> none  [body(): pl.pallas_call(hand_out, out_shape=(jax.ShapeDtypeStruct(primal.shape, F3...]
    pallas_call x1, Pallas kernels: 39.6 us -> 37.8 us  [body(): pl.pallas_call(functools.partial(kernel, n_row, n_col), out_shape=(jax.Sh...]
    unnamed x0 -> x2, local copies, waits for them, and re-layouts: none -> 1.23 us
where the time goes in v4:
time: 40.5 us; the launch traced here: 40.4 us
  Pallas kernels  37.8 us (93%)
  between operations  1.29 us (3%)
  local copies, waits for them, and re-layouts  1.23 us (3%)
    pallas_call x1, Pallas kernels, body(): pl.pallas_call(functools.partial(kernel, n_row, n_col), out_shape=(jax.Sh...  37.8 us
    unnamed x2, local copies, waits for them, and re-layouts  1.23 us

profile of v4, /device:TPU:0, one launch (start us, length us, event | category | flops | bytes accessed | tf_op | source)
XLA Modules:
  0.0 40.4 jit_solution(7764020373570914540)
XLA Ops:
  1.3 37.8 %pdhg.1 = (f32[8,1024]{1,0:T(8,128)S(1)}, f32[8,1024]{1,0:T(8,128)S(1)}) custom-call(f32[8,1024]{1,0:T(8,128)} %primal_h.1, f32[8,1024]{1,0:T(8,128)} %dual_h.1, f32[8,1024]{1,0:T(8,128)} %cost_h.1, f32[1,1024]{1,0:T(1,128)} %bitcast.5, f32[1,1024]{1,0:T(1,128)} %bitcast.6, s32[1,1024]{1,0:T(1,128)} %bitcast.7, bf16[48,128,128]{2,1,0:T(8,128)(2,1)} %tiles_h.1, ...), custom_call_target="tpu_custom_call" | custom-call | tf_op jit(solution)/shard_map/pdhg/pallas_call | solution.py:272
  39.1 0.6 %copy.15 = f32[8,1024]{1,0:T(8,128)} copy(f32[8,1024]{1,0:T(8,128)S(1)} %get-tuple-element.4) | data formatting | bytes 65536
  39.7 0.6 %copy.16 = f32[8,1024]{1,0:T(8,128)} copy(f32[8,1024]{1,0:T(8,128)S(1)} %get-tuple-element.5) | data formatting | bytes 65536

commit v5 on v4

--- a/solution.py
+++ b/solution.py
@@ -8,8 +8,8 @@
 from jax.sharding import PartitionSpec as P
 
 ITERS = 2
-GROUPS = 2
-HALF = 4
+GROUPS = 4
+HALF = 2
 PRIMAL_STEP = 0.4
 DUAL_STEP = 0.4
 BF16 = jnp.bfloat16
@@ -99,7 +99,7 @@
             source = lax.rem(me + n - d, n)
             fill(full, it, group, source * tiles, recv[it, group, d - 1].astype(F32), tiles)
 
-    upper_half = lax.broadcasted_iota(jnp.int32, (8, 128), 0) < HALF
+    upper_half = lax.broadcasted_iota(jnp.int32, (2 * HALF, 128), 0) < HALF
 
     def products(it, group, full, index, blocks):
         for s in range(0, slots, 2):
@@ -151,10 +151,10 @@
         sub = lax.broadcasted_iota(jnp.int32, (8, lanes), 0)
         own = lax.broadcasted_iota(jnp.int32, (8, lanes), 1) % HALF == sub % HALF
         place = jnp.where(own, place, -100000.0).astype(jnp.int32) - sub // HALF
-        two = jnp.concatenate([place, place - 2], axis=0)
+        two = jnp.concatenate([place, place - 8 // HALF], axis=0)
 
         def step(c, carry):
-            matrix[pl.ds(pl.multiple_of(c * 16, 16), 16), :] = jnp.where(two == 4 * c, 1.0, 0.0).astype(BF16)
+            matrix[pl.ds(pl.multiple_of(c * 16, 16), 16), :] = jnp.where(two == 16 // HALF * c, 1.0, 0.0).astype(BF16)
             return carry
 
         lax.fori_loop(0, matrix.shape[0] // 16, step, 0)
@@ -241,7 +241,7 @@
     def exchange(n, rows):
         return [
             pltpu.VMEM(both + (rows, 128), BF16), pltpu.VMEM(both + (n - 1, rows, 128), BF16),
-            pltpu.VMEM(both + (n * rows // HALF, 8, 128), F32),
+            pltpu.VMEM(both + (n * rows // HALF, 2 * HALF, 128), F32),
         ]
 
     def partial(n, rows):

time: 40.5 us -> 39.9 us (0.985)
  Pallas kernels: 37.8 us -> 37.2 us
    pallas_call x1, Pallas kernels: 37.8 us -> 37.2 us  [body(): pl.pallas_call(functools.partial(kernel, n_row, n_col), out_shape=(jax.Sh...]
where the time goes in v5:
time: 39.9 us; the launch traced here: 39.8 us
  Pallas kernels  37.2 us (93%)
  between operations  1.29 us (3%)
  local copies, waits for them, and re-layouts  1.23 us (3%)
    pallas_call x1, Pallas kernels, body(): pl.pallas_call(functools.partial(kernel, n_row, n_col), out_shape=(jax.Sh...  37.2 us
    unnamed x2, local copies, waits for them, and re-layouts  1.23 us

profile of v5, /device:TPU:0, one launch (start us, length us, event | category | flops | bytes accessed | tf_op | source)
XLA Modules:
  0.0 39.8 jit_solution(15558670285886201433)
XLA Ops:
  1.3 37.2 %pdhg.1 = (f32[8,1024]{1,0:T(8,128)S(1)}, f32[8,1024]{1,0:T(8,128)S(1)}) custom-call(f32[8,1024]{1,0:T(8,128)} %primal_h.1, f32[8,1024]{1,0:T(8,128)} %dual_h.1, f32[8,1024]{1,0:T(8,128)} %cost_h.1, f32[1,1024]{1,0:T(1,128)} %bitcast.5, f32[1,1024]{1,0:T(1,128)} %bitcast.6, s32[1,1024]{1,0:T(1,128)} %bitcast.7, bf16[48,128,128]{2,1,0:T(8,128)(2,1)} %tiles_h.1, ...), custom_call_target="tpu_custom_call" | custom-call | tf_op jit(solution)/shard_map/pdhg/pallas_call | solution.py:272
  38.5 0.6 %copy.15 = f32[8,1024]{1,0:T(8,128)} copy(f32[8,1024]{1,0:T(8,128)S(1)} %get-tuple-element.4) | data formatting | bytes 65536
  39.1 0.6 %copy.16 = f32[8,1024]{1,0:T(8,128)} copy(f32[8,1024]{1,0:T(8,128)S(1)} %get-tuple-element.5) | data formatting | bytes 65536

commit v6 on v5

--- a/solution.py
+++ b/solution.py
@@ -8,8 +8,8 @@
 from jax.sharding import PartitionSpec as P
 
 ITERS = 2
-GROUPS = 4
-HALF = 2
+GROUPS = 2
+HALF = 4
 PRIMAL_STEP = 0.4
 DUAL_STEP = 0.4
 BF16 = jnp.bfloat16
@@ -102,12 +102,26 @@
     upper_half = lax.broadcasted_iota(jnp.int32, (2 * HALF, 128), 0) < HALF
 
     def products(it, group, full, index, blocks):
-        for s in range(0, slots, 2):
-            one = jnp.where(upper_half, full[it, group, index[0, s]], 0.0)
-            two = jnp.where(upper_half, 0.0, full[it, group, index[0, s + 1]])
-            left = jnp.concatenate([one, two], axis=1).astype(BF16)
-            both = jnp.dot(left, blocks[s:s + 2].reshape(256, 128), preferred_element_type=F32)
-            contrib[group, s * HALF:(s + 2) * HALF, :] = both
+        zero = jnp.zeros((2 * HALF, 128), F32)
+        for s in range(0, slots, 4):
+            one = jnp.where(upper_half, full[it, group, index[0, s]], full[it, group, index[0, s + 1]])
+            two = jnp.where(upper_half, full[it, group, index[0, s + 2]], full[it, group, index[0, s + 3]])
+            left = jnp.concatenate(
+                [jnp.concatenate([one, zero], axis=0), jnp.concatenate([zero, two], axis=0)], axis=1
+            ).astype(BF16)
+            right = jnp.concatenate(
+                [
+                    jnp.concatenate([blocks[s], blocks[s + 2]], axis=0),
+                    jnp.concatenate([blocks[s + 1], blocks[s + 3]], axis=0),
+                ],
+                axis=1,
+            )
+            four = jnp.dot(left, right, preferred_element_type=F32)
+            for k in range(2):
+                half = four[2 * HALF * k:2 * HALF * (k + 1)]
+                contrib[group, (s + 2 * k) * HALF:(s + 2 * k + 2) * HALF, :] = jnp.where(
+                    upper_half, half[:, :128], half[:, 128:]
+                )
 
     def scatter_start(it, group, matrix, rows, send, recv, me, n, axis, s_sem, r_sem, narrow=False):
         terms = contrib[group]

time: 39.9 us -> 40.6 us (1.018)
  Pallas kernels: 37.2 us -> 37.9 us
    pallas_call x1, Pallas kernels: 37.2 us -> 37.9 us  [body(): pl.pallas_call(functools.partial(kernel, n_row, n_col), out_shape=(jax.Sh...]
where the time goes in v6:
time: 40.6 us; the launch traced here: 40.4 us
  Pallas kernels  37.9 us (93%)
  between operations  1.29 us (3%)
  local copies, waits for them, and re-layouts  1.23 us (3%)
    pallas_call x1, Pallas kernels, body(): pl.pallas_call(functools.partial(kernel, n_row, n_col), out_shape=(jax.Sh...  37.9 us
    unnamed x2, local copies, waits for them, and re-layouts  1.23 us

profile of v6, /device:TPU:0, one launch (start us, length us, event | category | flops | bytes accessed | tf_op | source)
XLA Modules:
  0.0 40.4 jit_solution(948917406062289503)
XLA Ops:
  1.3 37.9 %pdhg.1 = (f32[8,1024]{1,0:T(8,128)S(1)}, f32[8,1024]{1,0:T(8,128)S(1)}) custom-call(f32[8,1024]{1,0:T(8,128)} %primal_h.1, f32[8,1024]{1,0:T(8,128)} %dual_h.1, f32[8,1024]{1,0:T(8,128)} %cost_h.1, f32[1,1024]{1,0:T(1,128)} %bitcast.5, f32[1,1024]{1,0:T(1,128)} %bitcast.6, s32[1,1024]{1,0:T(1,128)} %bitcast.7, bf16[48,128,128]{2,1,0:T(8,128)(2,1)} %tiles_h.1, ...), custom_call_target="tpu_custom_call" | custom-call | tf_op jit(solution)/shard_map/pdhg/pallas_call | solution.py:286
  39.2 0.6 %copy.15 = f32[8,1024]{1,0:T(8,128)} copy(f32[8,1024]{1,0:T(8,128)S(1)} %get-tuple-element.4) | data formatting | bytes 65536
  39.8 0.6 %copy.16 = f32[8,1024]{1,0:T(8,128)} copy(f32[8,1024]{1,0:T(8,128)S(1)} %get-tuple-element.5) | data formatting | bytes 65536

commit v7 on v6

--- a/solution.py
+++ b/solution.py
@@ -8,8 +8,8 @@
 from jax.sharding import PartitionSpec as P
 
 ITERS = 2
-GROUPS = 2
-HALF = 4
+GROUPS = 4
+HALF = 2
 PRIMAL_STEP = 0.4
 DUAL_STEP = 0.4
 BF16 = jnp.bfloat16

time: 40.6 us -> 39.9 us (0.983)
  Pallas kernels: 37.9 us -> 37.2 us
    pallas_call x1, Pallas kernels: 37.9 us -> 37.2 us  [body(): pl.pallas_call(functools.partial(kernel, n_row, n_col), out_shape=(jax.Sh...]
where the time goes in v7:
time: 39.9 us; the launch traced here: 39.7 us
  Pallas kernels  37.2 us (93%)
  between operations  1.29 us (3%)
  local copies, waits for them, and re-layouts  1.23 us (3%)
    pallas_call x1, Pallas kernels, body(): pl.pallas_call(functools.partial(kernel, n_row, n_col), out_shape=(jax.Sh...  37.2 us
    unnamed x2, local copies, waits for them, and re-layouts  1.23 us

profile of v7, /device:TPU:0, one launch (start us, length us, event | category | flops | bytes accessed | tf_op | source)
XLA Modules:
  0.0 39.7 jit_solution(1493783290614825326)
XLA Ops:
  1.3 37.2 %pdhg.1 = (f32[8,1024]{1,0:T(8,128)S(1)}, f32[8,1024]{1,0:T(8,128)S(1)}) custom-call(f32[8,1024]{1,0:T(8,128)} %primal_h.1, f32[8,1024]{1,0:T(8,128)} %dual_h.1, f32[8,1024]{1,0:T(8,128)} %cost_h.1, f32[1,1024]{1,0:T(1,128)} %bitcast.5, f32[1,1024]{1,0:T(1,128)} %bitcast.6, s32[1,1024]{1,0:T(1,128)} %bitcast.7, bf16[48,128,128]{2,1,0:T(8,128)(2,1)} %tiles_h.1, ...), custom_call_target="tpu_custom_call" | custom-call | tf_op jit(solution)/shard_map/pdhg/pallas_call | solution.py:286
  38.5 0.6 %copy.15 = f32[8,1024]{1,0:T(8,128)} copy(f32[8,1024]{1,0:T(8,128)S(1)} %get-tuple-element.4) | data formatting | bytes 65536
  39.1 0.6 %copy.16 = f32[8,1024]{1,0:T(8,128)} copy(f32[8,1024]{1,0:T(8,128)S(1)} %get-tuple-element.5) | data formatting | bytes 65536
